TPU v7x, 32 devices: a whole 2x2x4 slice. The times are simulated.
32 devices in a mesh: seq: 8 (over y, x, core), head: 4 (over z).
Axes of the slice: x: 2, y: 2, z: 4, core: 2. Of those that a mesh axis runs over, the one named last changes fastest.
Arguments:
- d_bytes: bfloat16 [2048, 8192], P('seq', 'head'), may hold values from -6 to 6
- owner_groups: int32 [8, 8], replicated, may hold values from 0 to 63, as said below
- block_order: int32 [8], replicated, may hold values from 0 to 7, each once
- y_in: bfloat16 [2048, 4096], P('seq'), may hold values from -0.29882812 to 0.29882812
- w_proj: bfloat16 [4096, 8192], P('seq', 'head'), may hold values from -0.0625 to 0.0625
- w_out: bfloat16 [2048, 4096], P('head', 'seq'), may hold values from -0.125 to 0.125
- queries: bfloat16 [2048, 2048], P('seq', 'head'), may hold values from -24 to 24
- keys: bfloat16 [2048, 2048], P('seq', 'head'), may hold values from -24 to 24
- values: bfloat16 [2048, 2048], P('seq', 'head'), may hold values from -6 to 6
- attn_out: bfloat16 [2048, 2048], P('seq', 'head'), may hold values from -0.59765625 to 0.59765625
Outputs:
- layer_grad: bfloat16 [2048, 4096], P('seq', 'head')
- grad_proj: bfloat16 [4096, 8192], P('seq', 'head')
- grad_out: bfloat16 [2048, 4096], P('head', 'seq')
- grad_queries: bfloat16 [2048, 2048], P('seq', 'head')
- grad_keys: bfloat16 [2048, 2048], P('seq', 'head')
- grad_values: bfloat16 [2048, 2048], P('seq', 'head')
Inputs may be any that keep to these rules, and one draw needn't show every extreme that they name: `owner_groups`: row o lists the patch groups held by owner o; it holds exactly one group of every seq shard (group g covers patches g * 32 to g * 32 + 31, shard g // 8), and every group appears once. `block_order`: A permutation.
All inputs are finite; a program needn't handle non-finite values.
Results may differ from a plain program's by a relative error of at most 0.03.
Values may be sent and summed in bfloat16 or wider, within the bound.
A program may use at most 128 MiB of HBM per device.

v0:
```python
import math

import jax
import jax.numpy as jnp
from jax import lax
from jax.sharding import PartitionSpec as P

HEAD_DIM = 128


def body(d_bytes, owner_groups, block_order, y_in, w_proj, w_out, queries, keys, values, attn_out):
    flt = jnp.float32
    half = jnp.bfloat16
    owners = lax.axis_size("seq")
    splits = lax.axis_size("head")
    seq_index = lax.axis_index("seq")
    head_index = lax.axis_index("head")
    patch_dev = y_in.shape[0]
    model_w = y_in.shape[1]
    group_rows = patch_dev // owners
    columns = d_bytes.shape[1]
    owner_ids = jnp.arange(owners, dtype=jnp.int32)
    all_owned = lax.all_gather(d_bytes, "seq", axis=0, tiled=True)
    inverse = jnp.argsort(owner_groups.reshape(-1))
    natural_all = jnp.take(
        all_owned.reshape(owners * owners, group_rows, columns), inverse, axis=0
    ).reshape(owners * patch_dev, columns)
    natural = lax.dynamic_slice_in_dim(natural_all, seq_index * patch_dev, patch_dev, 0)
    y_all = lax.all_to_all(y_in, "seq", split_axis=1, concat_axis=0, tiled=True)
    grad_proj = lax.dot_general(
        y_all, natural_all, (((0,), (0,)), ((), ())), preferred_element_type=flt
    ).astype(half)
    head_part = lax.dot_general(
        natural,
        lax.all_gather(w_proj, "seq", axis=0, tiled=True),
        (((1,), (1,)), ((), ())),
        preferred_element_type=flt,
    )
    feature_dev = model_w // splits
    full_grad = lax.psum(head_part.astype(jnp.bfloat16), "head").astype(jnp.float32).astype(half)
    layer_grad = lax.dynamic_slice_in_dim(full_grad, head_index * feature_dev, feature_dev, 1)
    width_dev = queries.shape[1]
    attn_grad = lax.dot_general(
        full_grad,
        lax.all_gather(w_out, "seq", axis=1, tiled=True),
        (((1,), (1,)), ((), ())),
        preferred_element_type=flt,
    ).astype(half)
    out_term = lax.dot_general(
        attn_out, full_grad, (((0,), (0,)), ((), ())), preferred_element_type=flt
    )
    grad_out = (
        lax.psum_scatter(out_term.astype(jnp.bfloat16), "seq", scatter_dimension=1, tiled=True)
        .astype(jnp.float32)
        .astype(half)
    )
    heads_dev = width_dev // HEAD_DIM
    scale = 1.0 / math.sqrt(HEAD_DIM)
    query_heads = queries.reshape(patch_dev, heads_dev, HEAD_DIM)
    grad_heads = attn_grad.reshape(patch_dev, heads_dev, HEAD_DIM)
    delta = jnp.sum(
        grad_heads.astype(flt) * attn_out.reshape(patch_dev, heads_dev, HEAD_DIM).astype(flt),
        axis=2,
    ).T
    local_rows = jnp.arange(patch_dev, dtype=jnp.int32)
    my_block = jnp.sum(jnp.where(owner_ids == seq_index, block_order, 0))
    query_pos = my_block * patch_dev + local_rows
    keys_all, values_all = (
        lax.all_gather(keys, "seq", axis=0, tiled=True),
        lax.all_gather(values, "seq", axis=0, tiled=True),
    )
    all_rows = keys_all.shape[0]
    block_rows = math.gcd(512, all_rows)
    block_count = all_rows // block_rows
    row_ids = jnp.arange(all_rows, dtype=jnp.int32)
    row_owner = row_ids // patch_dev
    key_pos = (
        jnp.sum(
            jnp.where(row_owner[:, None] == owner_ids[None, :], block_order[None, :], 0), axis=1
        )
        * patch_dev
        + row_ids % patch_dev
    )
    key_blocks = keys_all.reshape(block_count, block_rows, heads_dev, HEAD_DIM)
    value_blocks = values_all.reshape(block_count, block_rows, heads_dev, HEAD_DIM)
    pos_blocks = key_pos.reshape(block_count, block_rows)

    def scores_of(key_block, pos_block):
        scores = (
            jnp.einsum("qhd,khd->hqk", query_heads, key_block, preferred_element_type=flt) * scale
        )
        allowed = pos_block[None, :] <= query_pos[:, None]
        return (scores, allowed)

    def statistics(running, pieces):
        highest, totals = running
        key_block, pos_block = pieces
        scores, allowed = scores_of(key_block, pos_block)
        scores = jnp.where(allowed[None], scores, -1e30)
        new_high = jnp.maximum(highest, jnp.max(scores, axis=2))
        weights = jnp.where(allowed[None], jnp.exp(scores - new_high[:, :, None]), 0.0)
        totals = totals * jnp.exp(highest - new_high) + jnp.sum(weights, axis=2)
        return ((new_high, totals), None)

    start_stats = (
        jnp.full((heads_dev, patch_dev), -1e30, flt),
        jnp.zeros((heads_dev, patch_dev), flt),
    )
    (highest, totals), _ = lax.scan(statistics, start_stats, (key_blocks, pos_blocks))
    log_total = highest + jnp.log(totals)

    def backward(grad_query, pieces):
        key_block, value_block, pos_block = pieces
        scores, allowed = scores_of(key_block, pos_block)
        weights = jnp.where(allowed[None], jnp.exp(scores - log_total[:, :, None]), 0.0)
        grad_weights = jnp.einsum(
            "qhd,khd->hqk", grad_heads, value_block, preferred_element_type=flt
        )
        grad_scores = (weights * (grad_weights - delta[:, :, None]) * scale).astype(half)
        weights_low = weights.astype(half)
        grad_query = grad_query + jnp.einsum(
            "hqk,khd->qhd", grad_scores, key_block, preferred_element_type=flt
        )
        key_term = jnp.einsum("hqk,qhd->khd", grad_scores, query_heads, preferred_element_type=flt)
        value_term = jnp.einsum("hqk,qhd->khd", weights_low, grad_heads, preferred_element_type=flt)
        return (grad_query, (key_term, value_term))

    start_grad = jnp.zeros((patch_dev, heads_dev, HEAD_DIM), flt)
    grad_query, (key_terms, value_terms) = lax.scan(
        backward, start_grad, (key_blocks, value_blocks, pos_blocks)
    )
    key_terms = key_terms.reshape(all_rows, width_dev)
    value_terms = value_terms.reshape(all_rows, width_dev)
    grad_keys, grad_values = (
        lax.psum_scatter(
            key_terms.astype(jnp.bfloat16), "seq", scatter_dimension=0, tiled=True
        ).astype(jnp.float32),
        lax.psum_scatter(
            value_terms.astype(jnp.bfloat16), "seq", scatter_dimension=0, tiled=True
        ).astype(jnp.float32),
    )
    grad_queries = grad_query.reshape(patch_dev, width_dev).astype(half)
    return (
        layer_grad,
        grad_proj,
        grad_out,
        grad_queries,
        grad_keys.astype(half),
        grad_values.astype(half),
    )


def solution(mesh):
    placed = (
        P("seq", "head"),
        P(),
        P(),
        P("seq", None),
        P("seq", "head"),
        P("head", "seq"),
        P("seq", "head"),
        P("seq", "head"),
        P("seq", "head"),
        P("seq", "head"),
    )
    return jax.shard_map(
        body,
        mesh=mesh,
        in_specs=placed,
        out_specs=(
            P("seq", "head"),
            P("seq", "head"),
            P("head", "seq"),
            P("seq", "head"),
            P("seq", "head"),
            P("seq", "head"),
        ),
        check_vma=False,
    )
```

profile of v0, /device:TPU:0, one launch (start us, length us, event | category | flops | bytes accessed | tf_op | source)
XLA Modules:
  0.0 512.7 jit_solution(13498672416140843091)
XLA Ops:
  7.2 0.7 all-gather.10.cloned.1.call-update
  8.0 0.7 all-gather.6.cloned.1.call-update
  8.7 0.7 all-gather.8.cloned.1.call-update
  10.8 2.0 sort.17
  13.2 0.6 fusion.31
  15.0 25.5 %all-gather.10.cloned.1.call-done = bf16[2048,512]{1,0:T(8,128)(2,1)} async-done(((bf16[256,512]{1,0:T(8,128)(2,1)}), bf16[2048,512]{1,0:T(8,128)(2,1)}) %all-gather.10.cloned.1.call-update) | async-done | bytes 2097168 | tf_op jit(solution)/shard_map/all_gather | solution.py:69
  40.5 2.5 reshape.160
  43.1 1.7 copy.78
  44.8 52.1 %all-gather.6.cloned.1.call-done = bf16[2048,2048]{1,0:T(8,128)(2,1)} async-done(((bf16[256,2048]{1,0:T(8,128)(2,1)}), bf16[2048,2048]{1,0:T(8,128)(2,1)}) %all-gather.6.cloned.1.call-update) | async-done | bytes 8388624 | tf_op jit(solution)/shard_map/all_gather | solution.py:23
  96.9 9.1 %gather_fusion = bf16[64,32,2048]{2,1,0:T(8,128)(2,1)} fusion(bf16[64,32,2048]{2,1,0:T(8,128)(2,1)} %bitcast.128, s32[1024]{0:T(1024)S(1)} %pad_clamp_fusion), kind=kCustom, calls=%fused_computation | custom fusion | bytes 16777472 | tf_op jit(solution)/shard_map/jit(_take)/gather | solution.py:25
  105.9 82.7 %all-gather.8.cloned.1.call-done = bf16[4096,2048]{1,0:T(8,128)(2,1)} async-done(((bf16[512,2048]{1,0:T(8,128)(2,1)}), bf16[4096,2048]{1,0:T(8,128)(2,1)}) %all-gather.8.cloned.1.call-update) | async-done | bytes 16777232 | tf_op jit(solution)/shard_map/all_gather | solution.py:35
  188.6 12.1 %convolution_convert_fusion.1 = bf16[256,4096]{1,0:T(8,128)(2,1)} fusion(bf16[4096,2048]{1,0:T(8,128)(2,1)} %all-gather.8.cloned.1.call-done, bf16[2048,2048]{1,0:T(8,128)(2,1)} %bitcast.127, s32[]{:T(128)S(6)} %select_n.64, pred[256]{0:T(512)(128)(4,1)S(1)} %dynamic-slice), kind=kOutput, calls=%fused_computation.41 | convolution fusion | flops 4296540160 | bytes 19923204 | tf_op jit(solution)/shard_map/dot_general | solution.py:33
  200.8 9.2 %while.28 = (s32[]{:T(128)}, f32[4,256]{1,0:T(4,128)S(1)}, f32[4,256]{1,0:T(4,128)S(1)}, s32[4,512]{1,0:T(4,128)S(1)}, bf16[4,512,4,128]{3,1,2,0:T(8,128)(2,1)},...) while((s32[]{:T(128)}, f32[4,256]{1,0:T(4,128)S(1)}, ...), condition=%wide.region_8.9_spmd.clone, body=%wide.region_5.8_spmd.clone.sunk | while | flops 138548480 | bytes 5436016 | solution.py:109
  201.0 1.5 fusion.66
  202.5 0.5 select_reduce_fusion.3
  203.3 1.5 fusion.66
  205.6 1.5 fusion.66
  207.9 1.5 fusion.66
  210.0 8.3 %all-gather.12.cloned.1.call-done = bf16[2048,512]{1,0:T(8,128)(2,1)} async-done(((bf16[256,512]{1,0:T(8,128)(2,1)}), bf16[2048,512]{1,0:T(8,128)(2,1)}) %all-gather.12.cloned.1.call-update) | async-done | bytes 2097168 | tf_op jit(solution)/shard_map/all_gather | solution.py:70
  218.3 4.0 reshape.162
  222.3 35.2 %all-gather.14.cloned.1.call-done = bf16[512,4096]{1,0:T(8,128)(2,1)} async-done(((bf16[512,512]{1,0:T(8,128)(2,1)}), bf16[512,4096]{1,0:T(8,128)(2,1)}) %all-gather.14.cloned.1.call-update) | async-done | bytes 4194320 | tf_op jit(solution)/shard_map/all_gather | solution.py:45
  257.5 89.3 %all-reduce.2.cloned.1.call-done = bf16[256,4096]{1,0:T(8,128)(2,1)} async-done(((bf16[256,4096]{1,0:T(8,128)(2,1)}), bf16[256,4096]{1,0:T(8,128)(2,1)}) %all-reduce.2.cloned.1.call-update) | async-done | bytes 2097168 | tf_op jit(solution)/shard_map/psum | solution.py:40
  346.8 4.8 convolution_convert_fusion.3
  351.7 1.2 reshape.163
  352.8 1.7 copy_bitcast_fusion.4
  355.0 3.2 fusion.22
  358.5 33.9 %while.29 = (s32[]{:T(128)}, f32[256,4,128]{0,2,1:T(8,128)}, bf16[4,512,4,128]{3,1,2,0:T(8,128)(2,1)}, bf16[4,512,4,128]{3,1,2,0:T(8,128)(2,1)}, bf16[4,512,4,12...) while((s32[]{:T(128)}, f32[256,4,128]{0,2,1:T(8,128)}, ...), condition=%wide.region_11.12_spmd.clone, body=%wide.region_10.11_spmd.clone.sunk | while | flops 675676416 | bytes 18630868 | solution.py:129
  358.7 1.7 bitcast_select_fusion.3
  360.4 1.2 constant_dynamic-slice_fusion.9
  362.1 1.3 fusion.79
  363.3 2.2 fusion.78
  365.6 1.3 fusion.80
  367.0 1.7 bitcast_select_fusion.3
  368.7 1.3 constant_dynamic-slice_fusion.9
  370.5 1.2 fusion.79
  371.7 2.4 fusion.78
  374.1 1.3 fusion.80
  375.5 1.7 bitcast_select_fusion.3
  377.2 1.2 constant_dynamic-slice_fusion.9
  378.9 1.3 fusion.79
  380.2 2.4 fusion.78
  382.6 1.3 fusion.80
  384.0 1.7 bitcast_select_fusion.3
  385.7 1.3 constant_dynamic-slice_fusion.9
  387.4 1.2 fusion.79
  388.7 2.4 fusion.78
  391.1 1.3 fusion.80
  392.3 3.2 copy.84
  395.5 1.7 copy.101
  397.3 1.6 copy-done.4
  398.8 2.4 copy.73
  401.3 3.7 all-to-all-start
  405.0 3.2 copy.85
  408.2 1.7 copy.100
  410.0 21.6 %all-to-all-done = bf16[256,8,512]{0,2,1:T(8,128)(2,1)S(1)} async-done(((bf16[256,8,512]{0,2,1:T(8,128)(2,1)}), bf16[256,8,512]{0,2,1:T(8,128)(2,1)S(1)}, u32[]{:S(2)}, u32[]{:S(2)}) %all-to-all-start) | async-done | bytes 2097184 | tf_op jit(solution)/shard_map/all_to_all | solution.py:29
  431.6 2.4 copy.74
  434.0 7.6 %broadcast_select_fusion = bf16[64,32,2048]{2,1,0:T(8,128)(2,1)} fusion(bf16[64,32,2048]{2,1,0:T(8,128)(2,1)} %gather_fusion, pred[64]{0:T(512)(128)(4,1)S(1)} %compare_and_fusion), kind=kLoop, calls=%fused_computation.38 | loop fusion | flops 4194304 | bytes 16777280 | tf_op jit(solution)/shard_map/jit(_take)/select_n | solution.py:25
  441.6 8.4 %fusion.23 = bf16[512,2048]{0,1:T(8,128)(2,1)S(1)} fusion(bf16[2048,2048]{1,0:T(8,128)(2,1)} %bitcast.129, bf16[2048,512]{1,0:T(8,128)(2,1)S(1)} %bitcast.136), kind=kOutput, calls=%fused_computation.43 | convolution fusion | flops 4296015872 | bytes 12582912 | tf_op jit(solution)/shard_map/dot_general | solution.py:30
  450.1 2.4 copy.86
  452.5 0.8 copy.90
  453.3 1.9 constant_dynamic-slice_fusion.3
  455.2 2.0 copy.87
  457.2 3.4 reduce-scatter.6.cloned.1.call-done
  460.7 45.5 %reduce-scatter.8.cloned.1.call-done = bf16[256,512]{1,0:T(8,128)(2,1)} async-done(((bf16[2048,512]{1,0:T(8,128)(2,1)}), bf16[256,512]{1,0:T(8,128)(2,1)}) %reduce-scatter.8.cloned.1.call-update) | async-done | bytes 262160 | tf_op jit(solution)/shard_map/reduce_scatter | solution.py:138
  (115 shorter events, 7.9 us)
Async XLA Ops:
  7.2 3.5 copy-start.8
  7.2 5.8 %copy-start.6 = (bf16[256,512]{1,0:T(8,128)(2,1)S(1)}, bf16[256,512]{1,0:T(8,128)(2,1)}, u32[]{:S(2)}) copy-start(bf16[256,512]{1,0:T(8,128)(2,1)} %param.23) | copy-start | bytes 786436
  7.2 33.4 %all-gather.10.cloned.1.call-start = ((), (), s32[]{:S(2)}) async-start(), calls=%async_computation.8 | async-start | bytes 2359296 | tf_op jit(solution)/shard_map/all_gather | solution.py:69
  7.9 88.9 %all-gather.6.cloned.1.call-start = ((), (), s32[]{:S(2)}) async-start(), calls=%async_computation.4 | async-start | bytes 9437184 | tf_op jit(solution)/shard_map/all_gather | solution.py:23
  8.7 4.5 copy-start.9
  8.7 5.8 %copy-start.7 = (bf16[256,512]{1,0:T(8,128)(2,1)S(1)}, bf16[256,512]{1,0:T(8,128)(2,1)}, u32[]{:S(2)}) copy-start(bf16[256,512]{1,0:T(8,128)(2,1)} %param.20) | copy-start | bytes 786436
  8.7 180.0 %all-gather.8.cloned.1.call-start = ((), (), s32[]{:S(2)}) async-start(), calls=%async_computation.5 | async-start | bytes 18874368 | tf_op jit(solution)/shard_map/all_gather | solution.py:35
  9.4 208.9 %all-gather.12.cloned.1.call-start = ((), (), s32[]{:S(2)}) async-start(), calls=%async_computation.9 | async-start | bytes 2359296 | tf_op jit(solution)/shard_map/all_gather | solution.py:70
  10.0 247.5 %all-gather.14.cloned.1.call-start = ((), (), s32[]{:S(2)}) async-start(), calls=%async_computation.10 | async-start | bytes 4718592 | tf_op jit(solution)/shard_map/all_gather | solution.py:45
  10.6 336.3 %all-reduce.2.cloned.1.call-start = ((), (), s32[]{:S(2)}) async-start(), calls=%async_computation.6 | async-start | bytes 4194304 | tf_op jit(solution)/shard_map/psum | solution.py:40
  200.8 254.4 %reduce-scatter.4.cloned.1.call-start = ((), (), s32[]{:S(2)}) async-start(), calls=%async_computation.7 | async-start | bytes 4718592 | tf_op jit(solution)/shard_map/reduce_scatter | solution.py:53
  351.7 3.3 copy-start.3
  358.2 102.4 %reduce-scatter.6.cloned.1.call-start = ((), (), s32[]{:S(2)}) async-start(), calls=%async_computation.11 | async-start | bytes 2359296 | tf_op jit(solution)/shard_map/reduce_scatter | solution.py:135
  358.7 2.9 copy-start
  363.3 2.2 copy-start.1
  367.0 3.0 copy-start
  371.7 2.4 copy-start.1
  375.5 2.9 copy-start
  380.2 2.4 copy-start.1
  384.0 3.0 copy-start
  388.6 2.4 copy-start.1
  397.2 1.6 copy-start.4
  401.3 30.3 %all-to-all-start = ((bf16[256,8,512]{0,2,1:T(8,128)(2,1)}), bf16[256,8,512]{0,2,1:T(8,128)(2,1)S(1)}, u32[]{:S(2)}, u32[]{:S(2)}) async-start(bf16[256,8,512]{0,2,1:T(8,128)(2,1)} %bitcast.133), calls=%async_computation | async-start | bytes 4194304 | tf_op jit(solution)/shard_map/all_to_all | solution.py:29
  404.9 101.2 %reduce-scatter.8.cloned.1.call-start = ((), (), s32[]{:S(2)}) async-start(), calls=%async_computation.12 | async-start | bytes 2359296 | tf_op jit(solution)/shard_map/reduce_scatter | solution.py:138
  434.0 7.6 %copy-start.5 = (bf16[8,256,512]{2,1,0:T(8,128)(2,1)S(1)}, bf16[8,256,512]{2,1,0:T(8,128)(2,1)}, u32[]{:S(2)}) copy-start(bf16[8,256,512]{2,1,0:T(8,128)(2,1)} %copy.74) | copy-start | bytes 6291460
  450.1 2.4 copy-start.2
Sparse Core Ops, SparseCore 0:
  9.9 30.5 all-gather.9
  42.4 54.3 all-gather.5
  98.7 89.8 all-gather.7
  190.4 27.8 all-gather.11
  220.0 37.4 all-gather.13
  260.3 86.4 all-reduce.1
  358.4 50.2 reduce-scatter.3
  412.5 48.1 reduce-scatter.5
  464.9 41.2 reduce-scatter.7
where the time goes:
time: 514 us; the launch traced here: 513 us
  waiting for transfers between devices  367 us (71%)
  matrix products  62.8 us (12%)
  local copies, waits for them, and re-layouts  49.5 us (10%)
  between operations  14.7 us (3%)
  other arithmetic  14.2 us (3%)
    psum x1, waiting for transfers between devices, body(): lax.psum(head_part.astype(jnp.bfloat16), 'head').astype(jnp.float32)  89.3 us
    all_gather x1, waiting for transfers between devices, body(): lax.all_gather(w_proj, 'seq', axis=0, tiled=True)  82.7 us
    all_gather x1, waiting for transfers between devices, body(): all_owned = lax.all_gather(d_bytes, 'seq', axis=0, tiled=True)  52.1 us
    reduce_scatter x1, waiting for transfers between devices, body(): lax.psum_scatter(value_terms.astype(jnp.bfloat16), 'seq', scatter_dimensi...  45.5 us
    all_gather x1, waiting for transfers between devices, body(): lax.all_gather(w_out, 'seq', axis=1, tiled=True)  35.2 us
    all_gather x1, waiting for transfers between devices, body(): lax.all_gather(keys, 'seq', axis=0, tiled=True)  25.5 us
    all_to_all x1, waiting for transfers between devices, body(): y_all = lax.all_to_all(y_in, 'seq', split_axis=1, concat_axis=0, tiled=True)  21.6 us
    unnamed x26, local copies, waits for them, and re-layouts  15.6 us
  transfers between devices with their start and end apart: 10, of which 9 were waited for; matrix products, arithmetic and copies ran while one was open for 22% of the time, Pallas kernels for 0%

commit v1 on v0

v1 whole, which is shorter than its diff:
```python
import functools
import math

import jax
import jax.numpy as jnp
from jax import lax
from jax.experimental import pallas as pl
from jax.experimental.pallas import tpu as pltpu
from jax.sharding import PartitionSpec as P

HEAD_DIM = 128
MESH = pl.DeviceIdType.MESH
FLT = jnp.float32
HALF = jnp.bfloat16
ANY = pl.BlockSpec(memory_space=pl.ANY)
VMEM = pl.BlockSpec(memory_space=pltpu.VMEM)
SMEM = pl.BlockSpec(memory_space=pltpu.SMEM)
VMEM_LIMIT = 56 * 1024 * 1024


def greet(axes):
    barrier = pltpu.get_barrier_semaphore()
    count = 0
    for axis, size in axes:
        me = lax.axis_index(axis)
        for k in range(1, size):
            pl.semaphore_signal(
                barrier, inc=1, device_id={axis: lax.rem(me + k, size)}, device_id_type=MESH
            )
        count += size - 1
    pl.semaphore_wait(barrier, count)


def spread(stride, n, source, target, send, recv):
    me = lax.axis_index("seq")
    size = n // stride
    copies = []
    for k in range(1, size):
        dst = lax.rem(me // stride + k, size) * stride + lax.rem(me, stride)
        copy = pltpu.make_async_remote_copy(
            src_ref=source(dst),
            dst_ref=target,
            send_sem=send.at[k],
            recv_sem=recv.at[k],
            device_id={"seq": dst},
            device_id_type=MESH,
        )
        copy.start()
        copies.append(copy)
    own = pltpu.make_async_copy(source(me), target, recv.at[0])
    own.start()
    return copies + [own]


def gather_kernel(n, d_ref, out_ref, send, recv, pair_send, pair_recv):
    me = lax.axis_index("seq")
    chips = n // 2
    chip, core = me // 2, lax.rem(me, 2)
    other = chip * 2 + (1 - core)
    greet((("seq", n),))
    copies = spread(2, n, lambda dst: d_ref, out_ref.at[me], send, recv)

    def pass_on(k, source, slot):
        copy = pltpu.make_async_remote_copy(
            src_ref=source,
            dst_ref=out_ref.at[slot],
            send_sem=pair_send.at[k],
            recv_sem=pair_recv.at[k],
            device_id={"seq": other},
            device_id_type=MESH,
        )
        copy.start()
        return copy

    passed = [pass_on(0, d_ref, me)]
    for k in range(1, chips):
        copies[k - 1].wait_recv()
        slot = lax.rem(chip + chips - k, chips) * 2 + core
        passed.append(pass_on(k, out_ref.at[slot], slot))
    for copy in passed:
        copy.wait()
    for copy in copies[:-1]:
        copy.wait_send()
    copies[-1].wait()


def gather(d_bytes, n):
    chips = n // 2
    return pl.pallas_call(
        functools.partial(gather_kernel, n),
        out_shape=jax.ShapeDtypeStruct((n,) + d_bytes.shape, d_bytes.dtype),
        in_specs=[ANY],
        out_specs=ANY,
        scratch_shapes=[pltpu.SemaphoreType.DMA((chips,))] * 4,
        compiler_params=pltpu.CompilerParams(collective_id=1, has_side_effects=True),
    )(d_bytes)


def middle_kernel(
    n, splits, heads, chunks,
    part, y, q, k, v, o,
    grad, y_all, q_all, k_all, v_all, o_all, oq_all,
    outer_buf, pair_buf, middle_buf, total,
    y_s, y_r, q_s, q_r, k_s, k_r, v_s, v_r, o_s, o_r, p_s, p_r, a_s, a_r, b_s, b_r, c_s, c_r,
):
    me = lax.axis_index("seq")
    z = lax.axis_index("head")
    share = n // heads
    greet((("seq", n), ("head", splits)) if splits == 4 else (("seq", n),))
    rows = part.shape[0] // chunks
    inner = jnp.logical_and(z >= 1, z <= 2)
    outer = jnp.logical_not(inner)
    beside = (z // 2) * 2 + (1 - lax.rem(z, 2))
    across = 3 - z

    def send(source, target, s, r, c, to):
        here = pl.ds(c * rows, rows)
        return pltpu.make_async_remote_copy(
            src_ref=source.at[here],
            dst_ref=target.at[here],
            send_sem=s.at[c],
            recv_sem=r.at[c],
            device_id={"head": to},
            device_id_type=MESH,
        )

    line = splits == 4
    first = [send(part, outer_buf, a_s, a_r, c, beside) for c in range(chunks)]
    second = [send(pair_buf, middle_buf, b_s, b_r, c, across) for c in range(chunks)]
    third = [send(total, total, c_s, c_r, c, beside) for c in range(chunks)]

    if line:

        @pl.when(outer)
        def _():
            for copy in first:
                copy.start()

    width = y.shape[1] // n

    def columns(ref, size, index):
        return ref.at[:, pl.ds(pl.multiple_of(index * size, size), size)]

    copies = spread(share, n, lambda d: columns(q, HEAD_DIM, d // share), q_all.at[me // share], q_s, q_r)
    copies += spread(share, n, lambda d: columns(o, HEAD_DIM, d // share), oq_all.at[me // share], p_s, p_r)
    copies += spread(1, n, lambda d: o, o_all.at[me], o_s, o_r)
    copies += spread(1, n, lambda d: columns(k, HEAD_DIM, d // share), k_all.at[me], k_s, k_r)
    copies += spread(1, n, lambda d: columns(v, HEAD_DIM, d // share), v_all.at[me], v_s, v_r)
    copies += spread(1, n, lambda d: columns(y, width, d), y_all.at[me], y_s, y_r)

    if line:

        @pl.when(inner)
        def _():
            lag = 2
            for step in range(chunks + lag):
                if step < chunks:
                    here = pl.ds(step * rows, rows)
                    first[step].wait_recv()
                    pair_buf[here] = (part[here].astype(FLT) + outer_buf[here].astype(FLT)).astype(HALF)
                    second[step].start()
                if step >= lag:
                    c = step - lag
                    here = pl.ds(c * rows, rows)
                    second[c].wait_recv()
                    total[here] = (pair_buf[here].astype(FLT) + middle_buf[here].astype(FLT)).astype(HALF)
                    third[c].start()
            for c in range(chunks):
                second[c].wait_send()
                third[c].wait_send()

        @pl.when(outer)
        def _():
            for c in range(chunks):
                third[c].wait_recv()
            for c in range(chunks):
                first[c].wait_send()

        grad[...] = total[...]
    else:
        grad[...] = part[...]
    for copy in copies:
        copy.wait()


def middle(part, y, q, k, v, o, n, splits):
    heads = q.shape[1] // HEAD_DIM
    rows = y.shape[0]
    chunks = 8
    block = lambda m, w: jax.ShapeDtypeStruct((m, rows, w), HALF)
    dma = pltpu.SemaphoreType.DMA
    return pl.pallas_call(
        functools.partial(middle_kernel, n, splits, heads, chunks),
        out_shape=(
            jax.ShapeDtypeStruct(part.shape, HALF),
            block(n, y.shape[1] // n),
            block(heads, HEAD_DIM),
            block(n, HEAD_DIM),
            block(n, HEAD_DIM),
            block(n, o.shape[1]),
            block(heads, HEAD_DIM),
        ),
        in_specs=[VMEM] + [ANY] * 5,
        out_specs=[VMEM] + [ANY] * 6,
        scratch_shapes=[pltpu.VMEM(part.shape, HALF)] * 4
        + [dma((n,))] * 12
        + [dma((chunks,))] * 6,
        compiler_params=pltpu.CompilerParams(
            collective_id=2, has_side_effects=True, vmem_limit_bytes=VMEM_LIMIT
        ),
    )(part, y, q, k, v, o)


def scatter_kernel(n, share, a_ref, out_ref, send, recv):
    me = lax.axis_index("seq")
    greet((("seq", n),))

    def source(d):
        column = pl.ds(pl.multiple_of(d // share * HEAD_DIM, HEAD_DIM), HEAD_DIM)
        return a_ref.at[:, lax.rem(d, share), :, column]

    for copy in spread(1, n, source, out_ref.at[me], send, recv):
        copy.wait()


def scatter(partial, n, share):
    slots, rows = partial.shape[0], partial.shape[2]
    return pl.pallas_call(
        functools.partial(scatter_kernel, n, share),
        out_shape=jax.ShapeDtypeStruct((n, slots, rows, HEAD_DIM), HALF),
        in_specs=[ANY],
        out_specs=ANY,
        scratch_shapes=[pltpu.SemaphoreType.DMA((n,))] * 2,
        compiler_params=pltpu.CompilerParams(collective_id=3, has_side_effects=True),
    )(partial)


def return_kernel(
    n, share, per, dq, dk, dv, grad, dq_out, dk_out, dv_out, grad_out, q_s, q_r, k_s, k_r, v_s, v_r, g_s, g_r
):
    me = lax.axis_index("seq")
    c = lax.axis_index("head")
    greet((("seq", n),))
    slot = lax.rem(me, per)
    sends = me // per == c
    shares = []
    for k in range(1, n):
        dst = lax.rem(me + k, n)
        shares.append(
            pltpu.make_async_remote_copy(
                src_ref=grad.at[dst],
                dst_ref=grad_out.at[slot],
                send_sem=g_s.at[k],
                recv_sem=g_r.at[slot],
                device_id={"seq": dst},
                device_id_type=MESH,
            )
        )
    own = pltpu.make_async_copy(grad.at[me], grad_out.at[slot], g_s.at[0])

    @pl.when(sends)
    def _():
        own.start()
        for copy in shares:
            copy.start()

    copies = spread(share, n, lambda d: dq.at[d // share], dq_out.at[me // share], q_s, q_r)
    copies += spread(1, n, lambda d: dk.at[d], dk_out.at[me], k_s, k_r)
    copies += spread(1, n, lambda d: dv.at[d], dv_out.at[me], v_s, v_r)
    for copy in copies:
        copy.wait()

    @pl.when(sends)
    def _():
        own.wait()
        for copy in shares:
            copy.wait_send()

    for i in range(per):

        @pl.when(c * per + i != me)
        def _():
            pltpu.make_async_copy(grad.at[0], grad_out.at[i], g_r.at[i]).wait()


def send_back(dq, dk, dv, grad, n, share, splits):
    per = n // splits
    dma = pltpu.SemaphoreType.DMA
    return pl.pallas_call(
        functools.partial(return_kernel, n, share, per),
        out_shape=(
            jax.ShapeDtypeStruct(dq.shape, HALF),
            jax.ShapeDtypeStruct(dk.shape, HALF),
            jax.ShapeDtypeStruct(dv.shape, HALF),
            jax.ShapeDtypeStruct((per,) + grad.shape[1:], HALF),
        ),
        in_specs=[ANY] * 4,
        out_specs=[ANY] * 4,
        scratch_shapes=[dma((n,))] * 7 + [dma((per,))],
        compiler_params=pltpu.CompilerParams(collective_id=4, has_side_effects=True),
    )(dq, dk, dv, grad)


def fetch_natural(groups, d_ref, nat, sem):
    owners, slots = groups.shape
    size = nat.shape[0] // (owners * slots)

    @pl.loop(0, owners)
    def _(o):
        for j in range(slots):
            g = groups[o, j]
            pltpu.make_async_copy(
                d_ref.at[o, pl.ds(j * size, size)],
                nat.at[pl.ds(pl.multiple_of(g * size, size), size)],
                sem,
            ).start()


def natural_done(nat, sem):
    pltpu.make_async_copy(nat, nat, sem).wait()


def part_kernel(groups, d_ref, w, out, nat, sem):
    fetch_natural(groups, d_ref, nat, sem)
    natural_done(nat, sem)
    tile = 256

    @pl.loop(0, nat.shape[0] // tile)
    def _(i):
        here = pl.ds(pl.multiple_of(i * tile, tile), tile)
        out[here] = lax.dot_general(
            nat[here], w[...], (((1,), (1,)), ((), ())), preferred_element_type=FLT
        ).astype(HALF)


def proj_kernel(groups, d_ref, y, out, nat, sem):
    fetch_natural(groups, d_ref, nat, sem)
    natural_done(nat, sem)
    tile = 512

    @pl.loop(0, nat.shape[1] // tile)
    def _(i):
        here = pl.ds(pl.multiple_of(i * tile, tile), tile)
        out[:, here] = lax.dot_general(
            y[...], nat[:, here], (((0,), (0,)), ((), ())), preferred_element_type=FLT
        ).astype(HALF)


def with_natural(kernel, groups, d_all, other, out_shape):
    nat = (d_all.shape[0] * d_all.shape[1], d_all.shape[2])
    return pl.pallas_call(
        kernel,
        out_shape=jax.ShapeDtypeStruct(out_shape, HALF),
        in_specs=[SMEM, ANY, VMEM],
        out_specs=VMEM,
        scratch_shapes=[pltpu.VMEM(nat, HALF), pltpu.SemaphoreType.DMA],
        compiler_params=pltpu.CompilerParams(vmem_limit_bytes=VMEM_LIMIT),
    )(groups, d_all, other)


def attention_kernel(qpos, kpos, q, k, v, o, go, dq, dk, dv, dk_sum, dv_sum):
    j = pl.program_id(0)
    scale = 1.0 / math.sqrt(HEAD_DIM)

    @pl.when(j == 0)
    def _():
        dk_sum[...] = jnp.zeros_like(dk_sum)
        dv_sum[...] = jnp.zeros_like(dv_sum)

    g = jnp.sum(go[:, 0].astype(FLT), axis=0).astype(HALF)
    delta = jnp.sum(g.astype(FLT) * o[0].astype(FLT), axis=1, keepdims=True)
    rowwise = (((1,), (1,)), ((), ()))
    columnwise = (((0,), (0,)), ((), ()))
    s = lax.dot_general(q[0], k[...], rowwise, preferred_element_type=FLT) * scale
    s = jnp.where(kpos[...] <= qpos[0], s, -1e30)
    high = jnp.max(s, axis=1, keepdims=True)
    e = jnp.exp(s - high)
    p = e * (1.0 / jnp.sum(e, axis=1, keepdims=True))
    dp = lax.dot_general(g, v[...], rowwise, preferred_element_type=FLT)
    ds = (p * (dp - delta) * scale).astype(HALF)
    low = p.astype(HALF)
    dq[0] = jnp.dot(ds, k[...], preferred_element_type=FLT).astype(HALF)
    dk_sum[...] += lax.dot_general(ds, q[0], columnwise, preferred_element_type=FLT)
    dv_sum[...] += lax.dot_general(low, g, columnwise, preferred_element_type=FLT)

    @pl.when(j == pl.num_programs(0) - 1)
    def _():
        dk[...] = dk_sum[...].astype(HALF)
        dv[...] = dv_sum[...].astype(HALF)


def attention(qpos, kpos, q, k, v, o, go):
    slots, rows, _ = q.shape
    n = go.shape[0]
    every = k.shape
    block = pl.BlockSpec((1, rows, HEAD_DIM), lambda j: (j, 0, 0))
    whole = pl.BlockSpec(every, lambda j: (0, 0))
    return pl.pallas_call(
        attention_kernel,
        grid=(slots,),
        out_shape=(
            jax.ShapeDtypeStruct(q.shape, HALF),
            jax.ShapeDtypeStruct(every, HALF),
            jax.ShapeDtypeStruct(every, HALF),
        ),
        in_specs=[
            pl.BlockSpec((1, rows, 1), lambda j: (j, 0, 0)),
            pl.BlockSpec(kpos.shape, lambda j: (0, 0)),
            block,
            whole,
            whole,
            block,
            pl.BlockSpec((n, 1, rows, HEAD_DIM), lambda j: (0, j, 0, 0)),
        ],
        out_specs=[block, whole, whole],
        scratch_shapes=[pltpu.VMEM(every, FLT)] * 2,
        compiler_params=pltpu.CompilerParams(vmem_limit_bytes=VMEM_LIMIT),
    )(qpos, kpos, q, k, v, o, go)


def body(d_bytes, owner_groups, block_order, y_in, w_proj, w_out, queries, keys, values, attn_out):
    n = lax.axis_size("seq")
    splits = lax.axis_size("head")
    me = lax.axis_index("seq")
    rows, width = queries.shape
    heads = width // HEAD_DIM
    share = n // heads
    patches = n * rows
    features = w_proj.shape[0]

    d_all = gather(d_bytes, n)
    part = with_natural(part_kernel, owner_groups, d_all, w_proj, (patches, features))
    if splits != 4:
        part = lax.psum(part, "head")
    grad, y_all, q_all, k_all, v_all, o_all, oq_all = middle(
        part, y_in, queries, keys, values, attn_out, n, splits
    )
    partial = lax.dot_general(
        grad, w_out, (((1,), (1,)), ((), ())), preferred_element_type=FLT
    ).astype(HALF)
    go = scatter(partial.reshape(heads, share, rows, width), n, share)
    grad_out = lax.dot_general(
        o_all.reshape(patches, width), grad, (((0,), (0,)), ((), ())), preferred_element_type=FLT
    ).astype(HALF)
    grad_proj = with_natural(
        proj_kernel, owner_groups, d_all, y_all.reshape(patches, features), (features, d_bytes.shape[1])
    )
    pos = block_order[:, None] * rows + jnp.arange(rows, dtype=jnp.int32)[None, :]
    mine = lax.dynamic_index_in_dim(pos.reshape(heads, share, rows), lax.rem(me, share), 1, False)
    dq, dk, dv = attention(
        mine[:, :, None],
        pos.reshape(1, patches),
        q_all,
        k_all.reshape(patches, HEAD_DIM),
        v_all.reshape(patches, HEAD_DIM),
        oq_all,
        go,
    )
    dq, dk, dv, grad = send_back(
        dq,
        dk.reshape(n, rows, HEAD_DIM),
        dv.reshape(n, rows, HEAD_DIM),
        grad.reshape(n, rows, features),
        n,
        share,
        splits,
    )

    def together(terms):
        terms = terms.reshape(heads, share, rows, HEAD_DIM)
        total = jnp.sum(terms.astype(FLT), axis=1).astype(HALF)
        return total.transpose(1, 0, 2).reshape(rows, width)

    grad_queries = dq.transpose(1, 0, 2).reshape(rows, width)
    layer_grad = grad.transpose(1, 0, 2).reshape(rows, -1)
    return (layer_grad, grad_proj, grad_out, grad_queries, together(dk), together(dv))


def solution(mesh):
    placed = (
        P("seq", "head"),
        P(),
        P(),
        P("seq", None),
        P("seq", "head"),
        P("head", "seq"),
        P("seq", "head"),
        P("seq", "head"),
        P("seq", "head"),
        P("seq", "head"),
    )
    return jax.shard_map(
        body,
        mesh=mesh,
        in_specs=placed,
        out_specs=(
            P("seq", "head"),
            P("seq", "head"),
            P("head", "seq"),
            P("seq", "head"),
            P("seq", "head"),
            P("seq", "head"),
        ),
        check_vma=False,
    )
```

time: 514 us -> 243 us (0.47)
  waiting for transfers between devices: 367 us -> 0 us
  Pallas kernels: 0 us -> 229 us
  matrix products: 62.8 us -> 4.66 us
  local copies, waits for them, and re-layouts: 49.5 us -> 7.17 us
  between operations: 14.7 us -> 0.79 us
  other arithmetic: 14.2 us -> 1.01 us
    pallas_call x0 -> x7, Pallas kernels: none -> 229 us  [the longest x1 73.5 us: middle(): pl.pallas_call(functools.partial(middle_kernel, n, splits, heads, chunks)...]
    all_gather x5 -> x0, waiting for transfers between devices: 204 us -> none  [the longest x1 82.7 us: body(): lax.all_gather(w_proj, 'seq', axis=0, tiled=True)]
    psum x1 -> x0, waiting for transfers between devices: 89.3 us -> none  [body(): lax.psum(head_part.astype(jnp.bfloat16), 'head').astype(jnp.float32)]
    dot_general x28 -> x2, matrix products: 62.8 us -> 4.66 us  [the longest x1 2.59 us: body(): lax.dot_general(grad, w_out, (((1,), (1,)), ((), ())), preferred_element_...]
    reduce_scatter x3 -> x0, waiting for transfers between devices: 48.9 us -> none  [the longest x1 45.5 us: body(): lax.psum_scatter(value_terms.astype(jnp.bfloat16), 'seq', scatter_dimensi...]
    all_to_all x1 -> x0, waiting for transfers between devices: 21.6 us -> none  [body(): y_all = lax.all_to_all(y_in, 'seq', split_axis=1, concat_axis=0, tiled=True)]
    unnamed x26 -> x17, local copies, waits for them, and re-layouts: 15.6 us -> 4.18 us
    gather x1 -> x0, local copies, waits for them, and re-layouts: 9.06 us -> none  [body(): jnp.take(all_owned.reshape(owners * owners, group_rows, columns), inverse...]
  transfers between devices with their start and end apart: 10 -> 0, of which waited for: 9 -> 0; matrix products, arithmetic and copies ran while one was open for 22% -> 0% of each run, Pallas kernels for 0% -> 0%
where the time goes in v1:
time: 243 us
  Pallas kernels  229 us (94%)
  local copies, waits for them, and re-layouts  7.17 us (3%)
  matrix products  4.66 us (2%)
    pallas_call x1, Pallas kernels, middle(): pl.pallas_call(functools.partial(middle_kernel, n, splits, heads, chunks)...  73.5 us
    pallas_call x1, Pallas kernels, gather(): pl.pallas_call(functools.partial(gather_kernel, n), out_shape=jax.ShapeDt...  55 us
    pallas_call x1, Pallas kernels, send_back(): pl.pallas_call(functools.partial(return_kernel, n, share, per), out_shape...  40.7 us
    pallas_call x1, Pallas kernels, scatter(): pl.pallas_call(functools.partial(scatter_kernel, n, share), out_shape=jax...  25 us
    pallas_call x2, Pallas kernels, with_natural(): pl.pallas_call(kernel, out_shape=jax.ShapeDtypeStruct(out_shape, HALF), i...  24.1 us
    pallas_call x1, Pallas kernels, attention(): pl.pallas_call(attention_kernel, grid=(slots,), out_shape=(jax.ShapeDtype...  11.1 us

profile of v1, /device:TPU:0, one launch (start us, length us, event | category | flops | bytes accessed | tf_op | source)
XLA Modules:
  0.0 243.0 jit_solution(1110680176041800825)
XLA Ops:
  0.6 0.0 copy-start
  0.7 0.7 broadcast_multiply_fusion
  1.4 0.1 add.36
  1.5 0.1 copy.29
  1.6 0.1 fusion
  1.6 0.1 add_bitcast_fusion
  1.7 0.6 copy.39
  2.3 1.0 copy.30.qpos
  3.3 55.0 %shard_map.145.d_ref = bf16[8,256,2048]{2,1,0:T(8,128)(2,1)} custom-call(bf16[256,2048]{1,0:T(8,128)(2,1)} %d_ref.1), custom_call_target="tpu_custom_call" | custom-call | tf_op jit(solution)/shard_map/pallas_call | solution.py:89
  58.3 12.3 %shard_map.146.part = bf16[2048,512]{1,0:T(8,128)(2,1)} custom-call(s32[8,8]{1,0:T(8,128)} %groups.3, bf16[8,256,2048]{2,1,0:T(8,128)(2,1)} %shard_map.145.d_ref, bf16[512,2048]{1,0:T(8,128)(2,1)} %w.1), custom_call_target="tpu_custom_call" | custom-call | tf_op jit(solution)/shard_map/pallas_call | solution.py:351
  70.6 73.5 %shard_map.147 = (bf16[2048,512]{1,0:T(8,128)(2,1)}, bf16[8,256,512]{2,1,0:T(8,128)(2,1)}, bf16[4,256,128]{2,1,0:T(8,128)(2,1)}, bf16[8,256,128]{2,1,0:T(8,128)(...) custom-call(bf16[2048,512]{1,0:T(8,128)(2,1)} %shard_map.146.part, ...), custom_call_target="tpu_custom_call" | custom-call | tf_op jit(solution)/shard_map/pallas_call | solution.py:192
  144.2 0.0 copy-start.1
  144.2 0.0 copy-start.2
  144.2 11.8 %shard_map.151 = bf16[512,2048]{1,0:T(8,128)(2,1)} custom-call(s32[8,8]{1,0:T(8,128)} %groups.3, bf16[8,256,2048]{2,1,0:T(8,128)(2,1)} %shard_map.145.d_ref, bf16[2048,512]{1,0:T(8,128)(2,1)} %bitcast.34), custom_call_target="tpu_custom_call" | custom-call | tf_op jit(solution)/shard_map/pallas_call | solution.py:351
  156.0 0.0 copy-done.1
  156.0 0.0 copy-done.2
  156.0 2.1 convolution_convert_fusion.1
  158.0 0.0 copy-done
  158.0 2.6 %convolution_convert_fusion = bf16[2048,512]{1,0:T(8,128)(2,1)} fusion(bf16[2048,512]{1,0:T(8,128)(2,1)S(1)} %copy-done.1, bf16[512,512]{1,0:T(8,128)(2,1)S(1)} %copy-done), kind=kOutput, calls=%fused_computation | convolution fusion | flops 1074790400 | bytes 4718592 | tf_op jit(solution)/shard_map/dot_general | solution.py:438
  160.6 25.0 %shard_map.148.go = bf16[8,4,256,128]{3,2,1,0:T(8,128)(2,1)} custom-call(bf16[4,2,256,512]{3,2,1,0:T(8,128)(2,1)} %bitcast.32), custom_call_target="tpu_custom_call" | custom-call | tf_op jit(solution)/shard_map/pallas_call | solution.py:228
  185.6 11.1 %shard_map.149 = (bf16[4,256,128]{2,1,0:T(8,128)(2,1)}, bf16[2048,128]{1,0:T(8,128)(2,1)}, bf16[2048,128]{1,0:T(8,128)(2,1)}) custom-call(s32[4,256,1]{2,1,0:T(8,128)} %copy.30.qpos, s32[1,2048]{1,0:T(1,128)} %bitcast.46, bf16[4,256,128]{2,1,0:T(8,128)(2,1)} %get-tuple-element.20.q, bf16[2048,128]{1,0:T(8,128)(2,1)} %bitcast.43, bf16[2048,128]{1,0:T(8,128)(2,1)} %bitcast.44, ...), custom_call_target="tpu_custom_call" | custom-call | tf_op jit(solution)/shard_map/pallas_call | solution.py:398
  196.8 40.7 %shard_map.150 = (bf16[4,256,128]{2,1,0:T(8,128)(2,1)}, bf16[8,256,128]{2,1,0:T(8,128)(2,1)}, bf16[8,256,128]{2,1,0:T(8,128)(2,1)}, bf16[2,256,512]{2,1,0:T(8,128)(2,1)}) custom-call(bf16[4,256,128]{2,1,0:T(8,128)(2,1)} %get-tuple-element.25.dq, bf16[8,256,128]{2,1,0:T(8,128)(2,1)} %bitcast.41, bf16[8,256,128]{2,1,0:T(8,128)(2,1)} %bitcast.42, ...), custom_call_target="tpu_custom_call" | custom-call | tf_op jit(solution)/shard_map/pallas_call | solution.py:289
  237.5 0.0 copy-start.5
  237.5 0.0 copy-start.3
  237.5 0.0 copy-start.4
  237.5 1.3 copy.31
  238.9 1.0 copy.35
  239.9 0.0 copy-done.5
  239.9 0.1 copy.32
  240.0 0.8 copy.36
  240.9 0.0 copy-done.3
  240.9 0.0 copy-done.4
  240.9 0.2 bitcast_reduce_fusion
  241.0 0.1 copy.34
  241.2 0.8 copy.38
  242.0 0.1 copy.33
  242.2 0.8 copy.37
  (1 shorter events, 0.0 us)
Async XLA Ops:
  0.6 157.4 %copy-start = (bf16[512,512]{1,0:T(8,128)(2,1)S(1)}, bf16[512,512]{1,0:T(8,128)(2,1)}, u32[]{:S(2)}) copy-start(bf16[512,512]{1,0:T(8,128)(2,1)} %param.15) | copy-start | bytes 1572868
  144.2 11.8 %copy-start.1 = (bf16[2048,512]{1,0:T(8,128)(2,1)S(1)}, bf16[2048,512]{1,0:T(8,128)(2,1)}, u32[]{:S(2)}) copy-start(bf16[2048,512]{1,0:T(8,128)(2,1)} %get-tuple-element.24) | copy-start | bytes 6291460
  144.2 11.8 %copy-start.2 = (bf16[8,256,512]{2,1,0:T(8,128)(2,1)S(1)}, bf16[8,256,512]{2,1,0:T(8,128)(2,1)}, u32[]{:S(2)}) copy-start(bf16[8,256,512]{2,1,0:T(8,128)(2,1)} %get-tuple-element.30) | copy-start | bytes 6291460
  237.5 2.4 copy-start.5
  237.5 3.4 %copy-start.3 = (bf16[8,256,128]{2,1,0:T(8,128)(2,1)S(1)}, bf16[8,256,128]{2,1,0:T(8,128)(2,1)}, u32[]{:S(2)}) copy-start(bf16[8,256,128]{2,1,0:T(8,128)(2,1)} %get-tuple-element.32) | copy-start | bytes 1572868
  237.5 3.4 %copy-start.4 = (bf16[8,256,128]{2,1,0:T(8,128)(2,1)S(1)}, bf16[8,256,128]{2,1,0:T(8,128)(2,1)}, u32[]{:S(2)}) copy-start(bf16[8,256,128]{2,1,0:T(8,128)(2,1)} %get-tuple-element.33) | copy-start | bytes 1572868

commit v2 on v1

--- a/solution.py
+++ b/solution.py
@@ -211,7 +211,7 @@
     )(part, y, q, k, v, o)
 
 
-def scatter_kernel(n, share, a_ref, out_ref, send, recv):
+def scatter_kernel(n, share, a_ref, nat_ref, y, out_ref, proj, nat, sem, send, recv):
     me = lax.axis_index("seq")
     greet((("seq", n),))
 
@@ -219,20 +219,39 @@
         column = pl.ds(pl.multiple_of(d // share * HEAD_DIM, HEAD_DIM), HEAD_DIM)
         return a_ref.at[:, lax.rem(d, share), :, column]
 
-    for copy in spread(1, n, source, out_ref.at[me], send, recv):
+    copies = spread(1, n, source, out_ref.at[me], send, recv)
+    fetch = pltpu.make_async_copy(nat_ref, nat, sem)
+    fetch.start()
+    fetch.wait()
+    tile = 512
+
+    @pl.loop(0, nat.shape[1] // tile)
+    def _(i):
+        here = pl.ds(pl.multiple_of(i * tile, tile), tile)
+        proj[:, here] = lax.dot_general(
+            y[...], nat[:, here], (((0,), (0,)), ((), ())), preferred_element_type=FLT
+        ).astype(HALF)
+
+    for copy in copies:
         copy.wait()
 
 
-def scatter(partial, n, share):
+def scatter(partial, natural, y, n, share):
     slots, rows = partial.shape[0], partial.shape[2]
     return pl.pallas_call(
         functools.partial(scatter_kernel, n, share),
-        out_shape=jax.ShapeDtypeStruct((n, slots, rows, HEAD_DIM), HALF),
-        in_specs=[ANY],
-        out_specs=ANY,
-        scratch_shapes=[pltpu.SemaphoreType.DMA((n,))] * 2,
-        compiler_params=pltpu.CompilerParams(collective_id=3, has_side_effects=True),
-    )(partial)
+        out_shape=(
+            jax.ShapeDtypeStruct((n, slots, rows, HEAD_DIM), HALF),
+            jax.ShapeDtypeStruct((y.shape[1], natural.shape[1]), HALF),
+        ),
+        in_specs=[ANY, ANY, VMEM],
+        out_specs=[ANY, VMEM],
+        scratch_shapes=[pltpu.VMEM(natural.shape, HALF), pltpu.SemaphoreType.DMA]
+        + [pltpu.SemaphoreType.DMA((n,))] * 2,
+        compiler_params=pltpu.CompilerParams(
+            collective_id=3, has_side_effects=True, vmem_limit_bytes=VMEM_LIMIT
+        ),
+    )(partial, natural, y)
 
 
 def return_kernel(
@@ -240,29 +259,46 @@
 ):
     me = lax.axis_index("seq")
     c = lax.axis_index("head")
-    greet((("seq", n),))
+    splits = n // per
     slot = lax.rem(me, per)
-    sends = me // per == c
-    shares = []
-    for k in range(1, n):
-        dst = lax.rem(me + k, n)
+    goal = me // per
+    base = lax.rem(c + splits - goal, splits)
+    barrier = pltpu.get_barrier_semaphore()
+    for i in range(splits):
+        for k in range(n):
+            if i + k > 0:
+                pl.semaphore_signal(
+                    barrier,
+                    inc=1,
+                    device_id={"seq": lax.rem(me + k, n), "head": lax.rem(c + i, splits)},
+                    device_id_type=MESH,
+                )
+    pl.semaphore_wait(barrier, n * splits - 1)
+    away, shares, own = [], [], []
+    for j in range(per):
+        dst = base + j * splits
+        away.append(jnp.logical_or(dst != me, goal != c))
         shares.append(
             pltpu.make_async_remote_copy(
                 src_ref=grad.at[dst],
                 dst_ref=grad_out.at[slot],
-                send_sem=g_s.at[k],
+                send_sem=g_s.at[j],
                 recv_sem=g_r.at[slot],
-                device_id={"seq": dst},
+                device_id={"seq": dst, "head": goal},
                 device_id_type=MESH,
             )
         )
-    own = pltpu.make_async_copy(grad.at[me], grad_out.at[slot], g_s.at[0])
-
-    @pl.when(sends)
-    def _():
-        own.start()
-        for copy in shares:
-            copy.start()
+        own.append(pltpu.make_async_copy(grad.at[dst], grad_out.at[slot], g_r.at[slot]))
+
+    for j in range(per):
+
+        @pl.when(away[j])
+        def _():
+            shares[j].start()
+
+        @pl.when(jnp.logical_not(away[j]))
+        def _():
+            own[j].start()
 
     copies = spread(share, n, lambda d: dq.at[d // share], dq_out.at[me // share], q_s, q_r)
     copies += spread(1, n, lambda d: dk.at[d], dk_out.at[me], k_s, k_r)
@@ -270,17 +306,14 @@
     for copy in copies:
         copy.wait()
 
-    @pl.when(sends)
-    def _():
-        own.wait()
-        for copy in shares:
-            copy.wait_send()
+    for j in range(per):
+
+        @pl.when(away[j])
+        def _():
+            shares[j].wait_send()
 
     for i in range(per):
-
-        @pl.when(c * per + i != me)
-        def _():
-            pltpu.make_async_copy(grad.at[0], grad_out.at[i], g_r.at[i]).wait()
+        pltpu.make_async_copy(grad.at[0], grad_out.at[i], g_r.at[i]).wait()
 
 
 def send_back(dq, dk, dv, grad, n, share, splits):
@@ -296,7 +329,7 @@
         ),
         in_specs=[ANY] * 4,
         out_specs=[ANY] * 4,
-        scratch_shapes=[dma((n,))] * 7 + [dma((per,))],
+        scratch_shapes=[dma((n,))] * 6 + [dma((per,))] * 2,
         compiler_params=pltpu.CompilerParams(collective_id=4, has_side_effects=True),
     )(dq, dk, dv, grad)
 
@@ -320,9 +353,11 @@
     pltpu.make_async_copy(nat, nat, sem).wait()
 
 
-def part_kernel(groups, d_ref, w, out, nat, sem):
+def part_kernel(groups, d_ref, w, out, nat_out, nat, sem):
     fetch_natural(groups, d_ref, nat, sem)
     natural_done(nat, sem)
+    keep = pltpu.make_async_copy(nat, nat_out, sem)
+    keep.start()
     tile = 256
 
     @pl.loop(0, nat.shape[0] // tile)
@@ -332,27 +367,16 @@
             nat[here], w[...], (((1,), (1,)), ((), ())), preferred_element_type=FLT
         ).astype(HALF)
 
-
-def proj_kernel(groups, d_ref, y, out, nat, sem):
-    fetch_natural(groups, d_ref, nat, sem)
-    natural_done(nat, sem)
-    tile = 512
-
-    @pl.loop(0, nat.shape[1] // tile)
-    def _(i):
-        here = pl.ds(pl.multiple_of(i * tile, tile), tile)
-        out[:, here] = lax.dot_general(
-            y[...], nat[:, here], (((0,), (0,)), ((), ())), preferred_element_type=FLT
-        ).astype(HALF)
+    keep.wait()
 
 
 def with_natural(kernel, groups, d_all, other, out_shape):
     nat = (d_all.shape[0] * d_all.shape[1], d_all.shape[2])
     return pl.pallas_call(
         kernel,
-        out_shape=jax.ShapeDtypeStruct(out_shape, HALF),
+        out_shape=(jax.ShapeDtypeStruct(out_shape, HALF), jax.ShapeDtypeStruct(nat, HALF)),
         in_specs=[SMEM, ANY, VMEM],
-        out_specs=VMEM,
+        out_specs=[VMEM, ANY],
         scratch_shapes=[pltpu.VMEM(nat, HALF), pltpu.SemaphoreType.DMA],
         compiler_params=pltpu.CompilerParams(vmem_limit_bytes=VMEM_LIMIT),
     )(groups, d_all, other)
@@ -429,7 +453,7 @@
     features = w_proj.shape[0]
 
     d_all = gather(d_bytes, n)
-    part = with_natural(part_kernel, owner_groups, d_all, w_proj, (patches, features))
+    part, natural = with_natural(part_kernel, owner_groups, d_all, w_proj, (patches, features))
     if splits != 4:
         part = lax.psum(part, "head")
     grad, y_all, q_all, k_all, v_all, o_all, oq_all = middle(
@@ -438,13 +462,12 @@
     partial = lax.dot_general(
         grad, w_out, (((1,), (1,)), ((), ())), preferred_element_type=FLT
     ).astype(HALF)
-    go = scatter(partial.reshape(heads, share, rows, width), n, share)
+    go, grad_proj = scatter(
+        partial.reshape(heads, share, rows, width), natural, y_all.reshape(patches, features), n, share
+    )
     grad_out = lax.dot_general(
         o_all.reshape(patches, width), grad, (((0,), (0,)), ((), ())), preferred_element_type=FLT
     ).astype(HALF)
-    grad_proj = with_natural(
-        proj_kernel, owner_groups, d_all, y_all.reshape(patches, features), (features, d_bytes.shape[1])
-    )
     pos = block_order[:, None] * rows + jnp.arange(rows, dtype=jnp.int32)[None, :]
     mine = lax.dynamic_index_in_dim(pos.reshape(heads, share, rows), lax.rem(me, share), 1, False)
     dq, dk, dv = attention(

time: 243 us -> 240 us (0.988)
  Pallas kernels: 229 us -> 222 us
    pallas_call x3 -> x2, Pallas kernels: 49.1 us -> 40.2 us  [the longest x1 27.9 us: scatter(): pl.pallas_call(functools.partial(scatter_kernel, n, share), out_shape=(ja...]
    unnamed x17 -> x14, local copies, waits for them, and re-layouts: 4.18 us -> 5.49 us
where the time goes in v2:
time: 240 us
  Pallas kernels  222 us (92%)
  local copies, waits for them, and re-layouts  8.42 us (4%)
  matrix products  7.04 us (3%)
    pallas_call x1, Pallas kernels, middle(): pl.pallas_call(functools.partial(middle_kernel, n, splits, heads, chunks)...  73.5 us
    pallas_call x1, Pallas kernels, gather(): pl.pallas_call(functools.partial(gather_kernel, n), out_shape=jax.ShapeDt...  55 us
    pallas_call x1, Pallas kernels, send_back(): pl.pallas_call(functools.partial(return_kernel, n, share, per), out_shape...  41.8 us
    pallas_call x1, Pallas kernels, scatter(): pl.pallas_call(functools.partial(scatter_kernel, n, share), out_shape=(ja...  27.9 us
    pallas_call x1, Pallas kernels, with_natural(): pl.pallas_call(kernel, out_shape=(jax.ShapeDtypeStruct(out_shape, HALF),...  12.3 us
    pallas_call x1, Pallas kernels, attention(): pl.pallas_call(attention_kernel, grid=(slots,), out_shape=(jax.ShapeDtype...  11.1 us
    unnamed x14, local copies, waits for them, and re-layouts  5.49 us

profile of v2, /device:TPU:0, one launch (start us, length us, event | category | flops | bytes accessed | tf_op | source)
XLA Modules:
  0.0 240.1 jit_solution(15609024863332809539)
XLA Ops:
  0.6 0.0 copy-start
  0.7 0.7 broadcast_multiply_fusion
  1.4 0.1 add.36
  1.5 0.1 copy.29
  1.6 0.1 fusion
  1.6 0.1 add_bitcast_fusion
  1.7 0.6 copy.39
  2.3 1.0 copy.30.qpos
  3.3 55.0 %shard_map.145.d_ref = bf16[8,256,2048]{2,1,0:T(8,128)(2,1)} custom-call(bf16[256,2048]{1,0:T(8,128)(2,1)} %d_ref.1), custom_call_target="tpu_custom_call" | custom-call | tf_op jit(solution)/shard_map/pallas_call | solution.py:89
  58.3 12.3 %shard_map.146 = (bf16[2048,512]{1,0:T(8,128)(2,1)}, bf16[2048,2048]{1,0:T(8,128)(2,1)}) custom-call(s32[8,8]{1,0:T(8,128)} %groups.1, bf16[8,256,2048]{2,1,0:T(8,128)(2,1)} %shard_map.145.d_ref, bf16[512,2048]{1,0:T(8,128)(2,1)} %w.1), custom_call_target="tpu_custom_call" | custom-call | tf_op jit(solution)/shard_map/pallas_call | solution.py:375
  70.7 73.5 %shard_map.147 = (bf16[2048,512]{1,0:T(8,128)(2,1)}, bf16[8,256,512]{2,1,0:T(8,128)(2,1)}, bf16[4,256,128]{2,1,0:T(8,128)(2,1)}, bf16[8,256,128]{2,1,0:T(8,128)(...) custom-call(bf16[2048,512]{1,0:T(8,128)(2,1)} %get-tuple-element.24.part, ...), custom_call_target="tpu_custom_call" | custom-call | tf_op jit(solution)/shard_map/pallas_call | solution.py:192
  144.1 0.0 copy-start.1
  144.2 4.4 %convolution_convert_fusion.1 = bf16[512,512]{1,0:T(8,128)(2,1)} fusion(bf16[2048,512]{1,0:T(8,128)(2,1)} %bitcast.31, bf16[2048,512]{1,0:T(8,128)(2,1)} %get-tuple-element.29), kind=kOutput, calls=%fused_computation.1 | convolution fusion | flops 1074003968 | bytes 4718592 | tf_op jit(solution)/shard_map/dot_general | solution.py:468
  148.6 0.0 copy-done
  148.6 0.0 copy-done.1
  148.6 2.6 %convolution_convert_fusion = bf16[2048,512]{1,0:T(8,128)(2,1)} fusion(bf16[2048,512]{1,0:T(8,128)(2,1)S(1)} %copy-done.1, bf16[512,512]{1,0:T(8,128)(2,1)S(1)} %copy-done), kind=kOutput, calls=%fused_computation | convolution fusion | flops 1074790400 | bytes 4718592 | tf_op jit(solution)/shard_map/dot_general | solution.py:462
  151.2 27.9 %shard_map.148 = (bf16[8,4,256,128]{3,2,1,0:T(8,128)(2,1)}, bf16[512,2048]{1,0:T(8,128)(2,1)}) custom-call(bf16[4,2,256,512]{3,2,1,0:T(8,128)(2,1)} %bitcast.34, bf16[2048,2048]{1,0:T(8,128)(2,1)} %get-tuple-element.30.nat_ref, bf16[2048,512]{1,0:T(8,128)(2,1)} %bitcast.33), custom_call_target="tpu_custom_call" | custom-call | tf_op jit(solution)/shard_map/pallas_call | solution.py:241
  179.1 11.1 %shard_map.149 = (bf16[4,256,128]{2,1,0:T(8,128)(2,1)}, bf16[2048,128]{1,0:T(8,128)(2,1)}, bf16[2048,128]{1,0:T(8,128)(2,1)}) custom-call(s32[4,256,1]{2,1,0:T(8,128)} %copy.30.qpos, s32[1,2048]{1,0:T(1,128)} %bitcast.46, bf16[4,256,128]{2,1,0:T(8,128)(2,1)} %get-tuple-element.25.q, bf16[2048,128]{1,0:T(8,128)(2,1)} %bitcast.43, bf16[2048,128]{1,0:T(8,128)(2,1)} %bitcast.44, ...), custom_call_target="tpu_custom_call" | custom-call | tf_op jit(solution)/shard_map/pallas_call | solution.py:422
  190.3 41.8 %shard_map.150 = (bf16[4,256,128]{2,1,0:T(8,128)(2,1)}, bf16[8,256,128]{2,1,0:T(8,128)(2,1)}, bf16[8,256,128]{2,1,0:T(8,128)(2,1)}, bf16[2,256,512]{2,1,0:T(8,128)(2,1)}) custom-call(bf16[4,256,128]{2,1,0:T(8,128)(2,1)} %get-tuple-element.33.dq, bf16[8,256,128]{2,1,0:T(8,128)(2,1)} %bitcast.41, bf16[8,256,128]{2,1,0:T(8,128)(2,1)} %bitcast.42, ...), custom_call_target="tpu_custom_call" | custom-call | tf_op jit(solution)/shard_map/pallas_call | solution.py:322
  232.1 0.0 copy-start.3
  232.1 1.3 copy.31
  233.4 1.0 copy.35
  234.4 0.0 copy-done.3
  234.4 0.1 copy.32
  234.6 0.0 copy-start.2
  234.6 0.8 copy.36
  235.4 1.4 bitcast_reduce_fusion
  236.8 0.1 copy.34
  236.9 0.8 copy.38
  237.8 0.1 copy.33
  237.9 0.8 copy.37
  238.8 0.0 copy-done.2
  238.8 1.3 copy.41
  (1 shorter events, 0.0 us)
Async XLA Ops:
  0.6 148.0 %copy-start = (bf16[512,512]{1,0:T(8,128)(2,1)S(1)}, bf16[512,512]{1,0:T(8,128)(2,1)}, u32[]{:S(2)}) copy-start(bf16[512,512]{1,0:T(8,128)(2,1)} %param.15) | copy-start | bytes 1572868
  144.1 4.5 %copy-start.1 = (bf16[2048,512]{1,0:T(8,128)(2,1)S(1)}, bf16[2048,512]{1,0:T(8,128)(2,1)}, u32[]{:S(2)}) copy-start(bf16[2048,512]{1,0:T(8,128)(2,1)} %get-tuple-element.29) | copy-start | bytes 6291460
  232.1 2.3 copy-start.3
  234.6 4.2 %copy-start.2 = (bf16[512,2048]{1,0:T(8,128)(2,1)S(1)}, bf16[512,2048]{1,0:T(8,128)(2,1)}, u32[]{:S(2)}) copy-start(bf16[512,2048]{1,0:T(8,128)(2,1)} %get-tuple-element.69) | copy-start | bytes 6291460

commit v3 on v2

--- a/solution.py
+++ b/solution.py
@@ -102,6 +102,7 @@
     grad, y_all, q_all, k_all, v_all, o_all, oq_all,
     outer_buf, pair_buf, middle_buf, total,
     y_s, y_r, q_s, q_r, k_s, k_r, v_s, v_r, o_s, o_r, p_s, p_r, a_s, a_r, b_s, b_r, c_s, c_r,
+    fo_s, fo_r, fk_s, fk_r, fv_s, fv_r,
 ):
     me = lax.axis_index("seq")
     z = lax.axis_index("head")
@@ -143,9 +144,32 @@
 
     copies = spread(share, n, lambda d: columns(q, HEAD_DIM, d // share), q_all.at[me // share], q_s, q_r)
     copies += spread(share, n, lambda d: columns(o, HEAD_DIM, d // share), oq_all.at[me // share], p_s, p_r)
-    copies += spread(1, n, lambda d: o, o_all.at[me], o_s, o_r)
-    copies += spread(1, n, lambda d: columns(k, HEAD_DIM, d // share), k_all.at[me], k_s, k_r)
-    copies += spread(1, n, lambda d: columns(v, HEAD_DIM, d // share), v_all.at[me], v_s, v_r)
+    chips = n // 2
+    chip, core = me // 2, lax.rem(me, 2)
+    other = chip * 2 + (1 - core)
+    head = me // share
+    shared = [
+        (o_all, o, lambda d: o, o_s, o_r, fo_s, fo_r),
+        (k_all, columns(k, HEAD_DIM, head), lambda d: columns(k, HEAD_DIM, d // share), k_s, k_r, fk_s, fk_r),
+        (v_all, columns(v, HEAD_DIM, head), lambda d: columns(v, HEAD_DIM, d // share), v_s, v_r, fv_s, fv_r),
+    ]
+
+    def pass_on(source, target, s, r, i):
+        copy = pltpu.make_async_remote_copy(
+            src_ref=source,
+            dst_ref=target,
+            send_sem=s.at[i],
+            recv_sem=r.at[i],
+            device_id={"seq": other},
+            device_id_type=MESH,
+        )
+        copy.start()
+        return copy
+
+    between, passed = [], []
+    for out, mine, source, s, r, fs, fr in shared:
+        between.append(spread(2, n, source, out.at[me], s, r))
+        passed.append(pass_on(mine, out.at[me], fs, fr, 0))
     copies += spread(1, n, lambda d: columns(y, width, d), y_all.at[me], y_s, y_r)
 
     if line:
@@ -179,7 +203,15 @@
         grad[...] = total[...]
     else:
         grad[...] = part[...]
-    for copy in copies:
+    for arrived, (out, _, _, _, _, fs, fr) in zip(between, shared):
+        for i in range(1, chips):
+            arrived[i - 1].wait_recv()
+            slot = lax.rem(chip + chips - i, chips) * 2 + core
+            passed.append(pass_on(out.at[slot], out.at[slot], fs, fr, i))
+        for copy in arrived[:-1]:
+            copy.wait_send()
+        arrived[-1].wait()
+    for copy in copies + passed:
         copy.wait()
 
 
@@ -204,7 +236,8 @@
         out_specs=[VMEM] + [ANY] * 6,
         scratch_shapes=[pltpu.VMEM(part.shape, HALF)] * 4
         + [dma((n,))] * 12
-        + [dma((chunks,))] * 6,
+        + [dma((chunks,))] * 6
+        + [dma((n // 2,))] * 6,
         compiler_params=pltpu.CompilerParams(
             collective_id=2, has_side_effects=True, vmem_limit_bytes=VMEM_LIMIT
         ),

time: 240 us -> 243 us (1.012)
  Pallas kernels: 222 us -> 225 us
    pallas_call x1, Pallas kernels: 73.5 us -> 76.4 us  [middle(): pl.pallas_call(functools.partial(middle_kernel, n, splits, heads, chunks)...]
where the time goes in v3:
time: 243 us
  Pallas kernels  225 us (93%)
  local copies, waits for them, and re-layouts  8.42 us (3%)
  matrix products  7.04 us (3%)
    pallas_call x1, Pallas kernels, middle(): pl.pallas_call(functools.partial(middle_kernel, n, splits, heads, chunks)...  76.4 us
    pallas_call x1, Pallas kernels, gather(): pl.pallas_call(functools.partial(gather_kernel, n), out_shape=jax.ShapeDt...  55 us
    pallas_call x1, Pallas kernels, send_back(): pl.pallas_call(functools.partial(return_kernel, n, share, per), out_shape...  41.8 us
    pallas_call x1, Pallas kernels, scatter(): pl.pallas_call(functools.partial(scatter_kernel, n, share), out_shape=(ja...  27.9 us
    pallas_call x1, Pallas kernels, with_natural(): pl.pallas_call(kernel, out_shape=(jax.ShapeDtypeStruct(out_shape, HALF),...  12.3 us
    pallas_call x1, Pallas kernels, attention(): pl.pallas_call(attention_kernel, grid=(slots,), out_shape=(jax.ShapeDtype...  11.1 us
    unnamed x14, local copies, waits for them, and re-layouts  5.49 us

profile of v3, /device:TPU:0, one launch (start us, length us, event | category | flops | bytes accessed | tf_op | source)
XLA Modules:
  0.0 243.0 jit_solution(2501834513123150367)
XLA Ops:
  0.6 0.0 copy-start
  0.7 0.7 broadcast_multiply_fusion
  1.4 0.1 add.36
  1.5 0.1 copy.29
  1.6 0.1 fusion
  1.6 0.1 add_bitcast_fusion
  1.7 0.6 copy.39
  2.3 1.0 copy.30.qpos
  3.3 55.0 %shard_map.145.d_ref = bf16[8,256,2048]{2,1,0:T(8,128)(2,1)} custom-call(bf16[256,2048]{1,0:T(8,128)(2,1)} %d_ref.1), custom_call_target="tpu_custom_call" | custom-call | tf_op jit(solution)/shard_map/pallas_call | solution.py:89
  58.3 12.3 %shard_map.146 = (bf16[2048,512]{1,0:T(8,128)(2,1)}, bf16[2048,2048]{1,0:T(8,128)(2,1)}) custom-call(s32[8,8]{1,0:T(8,128)} %groups.1, bf16[8,256,2048]{2,1,0:T(8,128)(2,1)} %shard_map.145.d_ref, bf16[512,2048]{1,0:T(8,128)(2,1)} %w.1), custom_call_target="tpu_custom_call" | custom-call | tf_op jit(solution)/shard_map/pallas_call | solution.py:408
  70.7 76.4 %shard_map.147 = (bf16[2048,512]{1,0:T(8,128)(2,1)}, bf16[8,256,512]{2,1,0:T(8,128)(2,1)}, bf16[4,256,128]{2,1,0:T(8,128)(2,1)}, bf16[8,256,128]{2,1,0:T(8,128)(...) custom-call(bf16[2048,512]{1,0:T(8,128)(2,1)} %get-tuple-element.24.part, ...), custom_call_target="tpu_custom_call" | custom-call | tf_op jit(solution)/shard_map/pallas_call | solution.py:224
  147.1 0.0 copy-start.1
  147.1 4.4 %convolution_convert_fusion.1 = bf16[512,512]{1,0:T(8,128)(2,1)} fusion(bf16[2048,512]{1,0:T(8,128)(2,1)} %bitcast.31, bf16[2048,512]{1,0:T(8,128)(2,1)} %get-tuple-element.29), kind=kOutput, calls=%fused_computation.1 | convolution fusion | flops 1074003968 | bytes 4718592 | tf_op jit(solution)/shard_map/dot_general | solution.py:501
  151.5 0.0 copy-done
  151.5 0.0 copy-done.1
  151.5 2.6 %convolution_convert_fusion = bf16[2048,512]{1,0:T(8,128)(2,1)} fusion(bf16[2048,512]{1,0:T(8,128)(2,1)S(1)} %copy-done.1, bf16[512,512]{1,0:T(8,128)(2,1)S(1)} %copy-done), kind=kOutput, calls=%fused_computation | convolution fusion | flops 1074790400 | bytes 4718592 | tf_op jit(solution)/shard_map/dot_general | solution.py:495
  154.1 27.9 %shard_map.148 = (bf16[8,4,256,128]{3,2,1,0:T(8,128)(2,1)}, bf16[512,2048]{1,0:T(8,128)(2,1)}) custom-call(bf16[4,2,256,512]{3,2,1,0:T(8,128)(2,1)} %bitcast.34, bf16[2048,2048]{1,0:T(8,128)(2,1)} %get-tuple-element.30.nat_ref, bf16[2048,512]{1,0:T(8,128)(2,1)} %bitcast.33), custom_call_target="tpu_custom_call" | custom-call | tf_op jit(solution)/shard_map/pallas_call | solution.py:274
  182.1 11.1 %shard_map.149 = (bf16[4,256,128]{2,1,0:T(8,128)(2,1)}, bf16[2048,128]{1,0:T(8,128)(2,1)}, bf16[2048,128]{1,0:T(8,128)(2,1)}) custom-call(s32[4,256,1]{2,1,0:T(8,128)} %copy.30.qpos, s32[1,2048]{1,0:T(1,128)} %bitcast.46, bf16[4,256,128]{2,1,0:T(8,128)(2,1)} %get-tuple-element.25.q, bf16[2048,128]{1,0:T(8,128)(2,1)} %bitcast.43, bf16[2048,128]{1,0:T(8,128)(2,1)} %bitcast.44, ...), custom_call_target="tpu_custom_call" | custom-call | tf_op jit(solution)/shard_map/pallas_call | solution.py:455
  193.2 41.8 %shard_map.150 = (bf16[4,256,128]{2,1,0:T(8,128)(2,1)}, bf16[8,256,128]{2,1,0:T(8,128)(2,1)}, bf16[8,256,128]{2,1,0:T(8,128)(2,1)}, bf16[2,256,512]{2,1,0:T(8,128)(2,1)}) custom-call(bf16[4,256,128]{2,1,0:T(8,128)(2,1)} %get-tuple-element.33.dq, bf16[8,256,128]{2,1,0:T(8,128)(2,1)} %bitcast.41, bf16[8,256,128]{2,1,0:T(8,128)(2,1)} %bitcast.42, ...), custom_call_target="tpu_custom_call" | custom-call | tf_op jit(solution)/shard_map/pallas_call | solution.py:355
  235.0 0.0 copy-start.3
  235.0 1.3 copy.31
  236.3 1.0 copy.35
  237.3 0.0 copy-done.3
  237.3 0.1 copy.32
  237.5 0.0 copy-start.2
  237.5 0.8 copy.36
  238.3 1.4 bitcast_reduce_fusion
  239.7 0.1 copy.34
  239.9 0.8 copy.38
  240.7 0.1 copy.33
  240.9 0.8 copy.37
  241.7 0.0 copy-done.2
  241.7 1.3 copy.41
  (1 shorter events, 0.0 us)
Async XLA Ops:
  0.6 150.9 %copy-start = (bf16[512,512]{1,0:T(8,128)(2,1)S(1)}, bf16[512,512]{1,0:T(8,128)(2,1)}, u32[]{:S(2)}) copy-start(bf16[512,512]{1,0:T(8,128)(2,1)} %param.15) | copy-start | bytes 1572868
  147.1 4.5 %copy-start.1 = (bf16[2048,512]{1,0:T(8,128)(2,1)S(1)}, bf16[2048,512]{1,0:T(8,128)(2,1)}, u32[]{:S(2)}) copy-start(bf16[2048,512]{1,0:T(8,128)(2,1)} %get-tuple-element.29) | copy-start | bytes 6291460
  235.0 2.3 copy-start.3
  237.5 4.2 %copy-start.2 = (bf16[512,2048]{1,0:T(8,128)(2,1)S(1)}, bf16[512,2048]{1,0:T(8,128)(2,1)}, u32[]{:S(2)}) copy-start(bf16[512,2048]{1,0:T(8,128)(2,1)} %get-tuple-element.69) | copy-start | bytes 6291460
